TPU v7x, 32 devices: a whole 2x2x4 slice. The times are simulated.
32 devices in a mesh: seq: 16 (over z, x, core), head: 2 (over y).
Axes of the slice: x: 2, y: 2, z: 4, core: 2. Of those that a mesh axis runs over, the one named last changes fastest.
Arguments:
- queries: bfloat16 [12288, 2048], P(('seq', 'head')), may hold values from -6 to 6
- keys: bfloat16 [12288, 2048], P(('seq', 'head')), may hold values from -6 to 6
- values: bfloat16 [12288, 2048], P(('seq', 'head')), may hold values from -6 to 6
- out_grad: bfloat16 [12288, 2048], P(('seq', 'head')), may hold values from -6 to 6
- window: int32 [16, 2], replicated, may hold values from 0 to 1, as said below
Outputs:
- grad_queries: bfloat16 [12288, 2048], P(('seq', 'head'))
- grad_keys: bfloat16 [12288, 2048], P(('seq', 'head'))
- grad_values: bfloat16 [12288, 2048], P(('seq', 'head'))
Inputs may be any that keep to these rules, and one draw needn't show every extreme that they name: `window`: some head reaches 1 along both time and height, some head 0 along both.
All inputs are finite; a program needn't handle non-finite values.
Results may differ from a plain program's by a relative error of at most 0.0066.
Values may be sent and summed in bfloat16 or wider, within the bound.
A program may use at most 192 MiB of HBM per device.

v0:
```python
import jax
import jax.numpy as jnp
from jax import lax
from jax.sharding import PartitionSpec as P

HD = 128
GH = 4


OFFSETS = tuple(((time_off, row_off) for time_off in (-1, 0, 1) for row_off in (-1, 0, 1)))


def passed_along(block, axis, distance):
    devices = range(lax.axis_size(axis))
    route = [(i - distance, i) for i in devices if i - distance in devices]
    return lax.ppermute(block, axis, route)


def shortened(array):

    def short(part):
        return part.astype(jnp.bfloat16) if part.dtype == jnp.float32 else part

    return jax.tree.map(short, array)


def neighbour_columns(payload):
    count = len(payload)
    columns = []
    for row_off in (-1, 0, 1):
        if row_off == 0:
            middle = payload
        else:
            middle = passed_along((payload[0], payload[1]), "seq", -row_off)
        far_ends = {}
        for time_off, pick in ((-1, 1), (1, 0)):
            far_ends[time_off] = passed_along(
                shortened(tuple((member[pick] for member in payload))),
                "seq",
                -(time_off * GH + row_off),
            )
        columns.append(
            tuple(
                (
                    jnp.concatenate(
                        [
                            far_ends[-1][member_num][None],
                            middle[member_num],
                            far_ends[1][member_num][None],
                        ],
                        axis=0,
                    )
                    for member_num in range(count)
                )
            )
        )
    return tuple(
        (jnp.stack([column[member_num] for column in columns]) for member_num in range(count))
    )


def column_windows(column):
    heads_here = column.shape[3]
    picked = jnp.stack([column[:, tile_num : tile_num + 3] for tile_num in (0, 1)])
    picked = jnp.transpose(picked, (0, 4, 2, 1, 3, 5))
    return picked.reshape(2 * heads_here, 9, column.shape[2], column.shape[4])


def terms_to_columns(terms, heads_here):
    shaped = terms.reshape(2, heads_here, 3, 3, terms.shape[2], terms.shape[3])
    shaped = jnp.transpose(shaped, (0, 3, 2, 4, 1, 5))
    first = jnp.pad(shaped[0], ((0, 0), (0, 1), (0, 0), (0, 0), (0, 0)))
    second = jnp.pad(shaped[1], ((0, 0), (1, 0), (0, 0), (0, 0), (0, 0)))
    return first + second


def to_items(tiles):
    return jnp.transpose(tiles, (0, 2, 1, 3)).reshape(
        2 * tiles.shape[2], tiles.shape[1], tiles.shape[3]
    )


def items_to_rows(items, heads_here):
    shaped = items.reshape(2, heads_here, items.shape[1], items.shape[2])
    return jnp.transpose(shaped, (0, 2, 1, 3)).reshape(
        2 * items.shape[1], heads_here * items.shape[2]
    )


def window_mask(window, heads_here):
    seq_index = lax.axis_index("seq")
    grid_time = 2 * (lax.axis_size("seq") // GH)
    slab_time = 2 * (seq_index // GH)
    tile_row = seq_index % GH
    reaches = lax.dynamic_slice_in_dim(window, lax.axis_index("head") * heads_here, heads_here, 0)
    per_tile = []
    for tile_num in (0, 1):
        columns = []
        for time_off, row_off in OFFSETS:
            near_time = slab_time + tile_num + time_off
            inside = (near_time >= 0) & (near_time < grid_time)
            inside = inside & (tile_row + row_off >= 0) & (tile_row + row_off < GH)
            allowed = inside & (abs(time_off) <= reaches[:, 0]) & (abs(row_off) <= reaches[:, 1])
            columns.append(allowed)
        per_tile.append(jnp.stack(columns, axis=1))
    return jnp.stack(per_tile).reshape(2 * heads_here, 9)


def query_core(query_head, grad_head, key_head, value_head, mask_row):
    score_scale = HD ** (-0.5)
    scores = (
        jnp.einsum("qd,okd->oqk", query_head, key_head, preferred_element_type=jnp.float32)
        * score_scale
    )
    scores = jnp.where(mask_row[:, None, None], scores, -jnp.inf)
    row_max = jnp.max(scores, axis=(0, 2))
    log_total = row_max + jnp.log(jnp.sum(jnp.exp(scores - row_max[None, :, None]), axis=(0, 2)))
    weights = jnp.exp(scores - log_total[None, :, None])
    grad_scores = jnp.einsum(
        "qd,okd->oqk", grad_head, value_head, preferred_element_type=jnp.float32
    )
    row_delta = jnp.sum(weights * grad_scores, axis=(0, 2))
    dscore = (weights * (grad_scores - row_delta[None, :, None])).astype(jnp.bfloat16)
    grad_query = (
        jnp.einsum("oqk,okd->qd", dscore, key_head, preferred_element_type=jnp.float32)
        * score_scale
    )
    return (weights.astype(jnp.bfloat16), dscore, log_total, row_delta, grad_query)


def query_with_terms(operands):
    query_head, grad_head, key_head, value_head, mask_row = operands
    rounded_probs, dscore, log_total, row_delta, grad_query = query_core(
        query_head, grad_head, key_head, value_head, mask_row
    )
    value_terms = jnp.einsum(
        "oqk,qd->okd", rounded_probs, grad_head, preferred_element_type=jnp.float32
    )
    key_terms = jnp.einsum(
        "oqk,qd->okd", dscore, query_head, preferred_element_type=jnp.float32
    ) * HD ** (-0.5)
    return (grad_query, key_terms, value_terms)


def per_device(queries, keys, values, out_grad, window):
    q_all, k_all, v_all, g_all = (
        lax.all_to_all(queries, "head", split_axis=1, concat_axis=0, tiled=True),
        lax.all_to_all(keys, "head", split_axis=1, concat_axis=0, tiled=True),
        lax.all_to_all(values, "head", split_axis=1, concat_axis=0, tiled=True),
        lax.all_to_all(out_grad, "head", split_axis=1, concat_axis=0, tiled=True),
    )
    tile_rows = q_all.shape[0] // 2
    heads_here = q_all.shape[1] // HD
    tile_shape = (2, tile_rows, heads_here, HD)
    q_here = q_all.reshape(tile_shape)
    k_here = k_all.reshape(tile_shape)
    v_here = v_all.reshape(tile_shape)
    g_here = g_all.reshape(tile_shape)
    visible = window_mask(window, heads_here)
    key_column, value_column = neighbour_columns((k_here, v_here))
    query_items = to_items(q_here)
    grad_items = to_items(g_here)
    operands = (
        query_items,
        grad_items,
        column_windows(key_column),
        column_windows(value_column),
        visible,
    )
    grad_query, key_terms, value_terms = lax.map(query_with_terms, operands)
    key_back = terms_to_columns(key_terms, heads_here)
    value_back = terms_to_columns(value_terms, heads_here)
    key_own = [key_back[1, 1], key_back[1, 2]]
    value_own = [value_back[1, 1], value_back[1, 2]]
    for row_off in (-1, 1):
        arrived_key, arrived_value = passed_along(
            (key_back[row_off + 1, 1:3], value_back[row_off + 1, 1:3]), "seq", row_off
        )
        for tile_num in (0, 1):
            key_own[tile_num] = key_own[tile_num] + arrived_key[tile_num]
            value_own[tile_num] = value_own[tile_num] + arrived_value[tile_num]
    for row_off in (-1, 0, 1):
        for time_off, place, target in ((-1, 0, 1), (1, 3, 0)):
            arrived_key, arrived_value = (
                passed_along(
                    key_back[row_off + 1, place].astype(jnp.bfloat16),
                    "seq",
                    time_off * GH + row_off,
                ).astype(jnp.float32),
                passed_along(
                    value_back[row_off + 1, place].astype(jnp.bfloat16),
                    "seq",
                    time_off * GH + row_off,
                ).astype(jnp.float32),
            )
            key_own[target] = key_own[target] + arrived_key
            value_own[target] = value_own[target] + arrived_value
    grad_keys = jnp.stack(key_own).reshape(2 * tile_rows, heads_here * HD).astype(jnp.bfloat16)
    grad_values = jnp.stack(value_own).reshape(2 * tile_rows, heads_here * HD).astype(jnp.bfloat16)
    grad_queries = items_to_rows(grad_query, heads_here).astype(jnp.bfloat16)
    return (
        lax.all_to_all(grad_queries, "head", split_axis=0, concat_axis=1, tiled=True),
        lax.all_to_all(grad_keys, "head", split_axis=0, concat_axis=1, tiled=True),
        lax.all_to_all(grad_values, "head", split_axis=0, concat_axis=1, tiled=True),
    )


def solution(mesh):
    return jax.shard_map(
        per_device,
        mesh=mesh,
        in_specs=(
            P(("seq", "head"), None),
            P(("seq", "head"), None),
            P(("seq", "head"), None),
            P(("seq", "head"), None),
            P(),
        ),
        out_specs=(P(("seq", "head"), None), P(("seq", "head"), None), P(("seq", "head"), None)),
        check_vma=False,
    )
```

profile of v0, /device:TPU:2, one launch (start us, length us, event | category | flops | bytes accessed | tf_op | source)
XLA Modules:
  0.0 822.2 jit_solution(15901379742496665024)
XLA Ops:
  8.6 17.9 %all-to-all-done.2 = bf16[384,2,1024]{0,2,1:T(8,128)(2,1)S(1)} async-done(((bf16[384,2,1024]{0,2,1:T(8,128)(2,1)}), bf16[384,2,1024]{0,2,1:T(8,128)(2,1)S(1)}, u32[]{:S(2)}, u32[]{:S(2)}) %all-to-all-start.2) | async-done | bytes 1572896 | tf_op jit(solution)/shard_map/all_to_all | solution.py:149
  32.8 5.4 collective-permute-start.11
  38.3 10.5 %all-to-all-done = bf16[384,2,1024]{0,2,1:T(8,128)(2,1)S(1)} async-done(((bf16[384,2,1024]{0,2,1:T(8,128)(2,1)}), bf16[384,2,1024]{0,2,1:T(8,128)(2,1)S(1)}, u32[]{:S(2)}, u32[]{:S(2)}) %all-to-all-start) | async-done | bytes 1572896 | tf_op jit(solution)/shard_map/all_to_all | solution.py:148
  54.7 6.4 collective-permute-start.3
  65.6 4.6 all-to-all-start.1
  72.0 7.0 collective-permute-start.5
  79.0 10.0 %collective-permute-done.4 = bf16[384,8,128]{0,2,1:T(8,128)(2,1)} collective-permute-done((bf16[384,8,128]{0,2,1:T(8,128)(2,1)}, bf16[384,8,128]{0,2,1:T(8,128)(2,1)}, u32[]{:S(2)}, u32[]{:S(2)}) %collective-permute-start.4) | collective-permute-done | bytes 786464 | tf_op jit(solution)/shard_map/ppermute | solution.py:16
  90.3 47.4 %collective-permute-start = (bf16[384,8,128]{0,2,1:T(8,128)(2,1)}, bf16[384,8,128]{0,2,1:T(8,128)(2,1)}, u32[]{:S(2)}, u32[]{:S(2)}) collective-permute-start(bf16[384,8,128]{0,2,1:T(8,128)(2,1)} %bitcast.18), channel_id=1, source_target_pairs={{0,10},{2,12},{4,14},{6,16},{8,18},{10,20},{12,22},{14,24},{16,26}... | collective-permute-start | bytes 2359304 | tf_op jit(solution)/shard_map/ppermute | solution.py:16
  150.3 4.0 maximum_bitcast_fusion.4
  154.3 6.1 collective-permute-start.13
  164.7 4.0 maximum_bitcast_fusion.2
  168.6 8.5 %pad_maximum_fusion = bf16[3,4,384,8,128]{2,4,3,1,0:T(8,128)(2,1)} fusion(bf16[1,4,384,8,128]{2,4,3,1,0:T(8,128)(2,1)} %maximum_bitcast_fusion.4, bf16[1,4,384,8,128]{2,4,3,1,0:T(8,128)(2,1)} %maximum_bitcast_fusion.3, bf16[1,4,384,8,128]{2,4,3,1,0:T(8,128)(2,1)} %maximum_bitcast_fusion.2), kind=kLoop, calls=%fused_computation.59 | loop fusion | flops 9437184 | bytes 18874368 | tf_op jit(solution)/shard_map/stack | solution.py:58
  177.1 6.7 slice_bitcast_fusion.7
  183.8 7.6 collective-permute-start.8
  191.4 5.9 maximum_bitcast_fusion
  197.2 18.7 %copy.127 = bf16[2,8,3,3,384,128]{5,4,3,2,1,0:T(8,128)(2,1)} copy(bf16[2,8,3,3,384,128]{4,5,1,2,3,0:T(8,128)(2,1)} %maximum_bitcast_fusion) | data formatting | bytes 28311552 | tf_op jit(solution)/shard_map/transpose | solution.py:65
  215.9 3.9 maximum_bitcast_fusion.7
  221.0 4.1 maximum_bitcast_fusion.5
  225.1 7.0 pad_maximum_fusion.1
  232.1 10.7 %slice_bitcast_fusion.5 = (bf16[1,3,3,384,8,128]{3,5,4,2,1,0:T(8,128)(2,1)}, bf16[1,3,3,384,8,128]{3,5,4,2,1,0:T(8,128)(2,1)}) fusion(bf16[3,4,384,8,128]{2,4,3,1,0:T(8,128)(2,1)} %pad_maximum_fusion.1), kind=kLoop, calls=%fused_computation.62 | loop fusion | bytes 28311552 | tf_op jit(solution)/shard_map/stack | solution.py:64
  242.8 3.9 all-to-all-start.3
  246.6 10.6 %maximum_bitcast_fusion.1 = bf16[2,8,3,3,384,128]{4,5,1,2,3,0:T(8,128)(2,1)} fusion(bf16[1,3,3,384,8,128]{3,5,4,2,1,0:T(8,128)(2,1)} %get-tuple-element.158, bf16[1,3,3,384,8,128]{3,5,4,2,1,0:T(8,128)(2,1)} %get-tuple-element.157), kind=kLoop, calls=%fused_computation.58 | loop fusion | flops 7077888 | bytes 28311552 | tf_op jit(solution)/shard_map/transpose | solution.py:65
  257.2 18.7 %copy.130 = bf16[2,8,3,3,384,128]{5,4,3,2,1,0:T(8,128)(2,1)} copy(bf16[2,8,3,3,384,128]{4,5,1,2,3,0:T(8,128)(2,1)} %maximum_bitcast_fusion.1) | data formatting | bytes 28311552 | tf_op jit(solution)/shard_map/transpose | solution.py:65
  276.0 236.7 %while.14 = (s32[]{:T(128)}, bf16[16,384,128]{2,1,0:T(8,128)(2,1)S(1)}, f32[16,9,384,128]{3,2,1,0:T(8,128)}, f32[16,9,384,128]{3,2,1,0:T(8,128)}, pred[16,9]{1,0...) while((s32[]{:T(128)}, ...), condition=%wide.region_4.5_spmd, body=%wide.region_0.4_spmd.sunk | while | flops 1728380160 | bytes 51928732 | solution.py:170
  513.9 9.9 %slice_bitcast_fusion.1 = (f32[3,3,384,8,128]{4,2,0,1,3:T(8,128)S(1)}, f32[3,3,384,8,128]{4,2,0,1,3:T(8,128)S(1)}) fusion(f32[2,3,3,384,8,128]{5,3,1,2,4,0:T(8,128)} %bitcast.338), kind=kLoop, calls=%fused_computation.54 | loop fusion | bytes 56623104 | tf_op jit(solution)/shard_map/squeeze | solution.py:72
  523.8 4.9 copy-done.4
  528.8 8.6 %pad_add_fusion = f32[3,4,384,8,128]{4,2,0,1,3:T(8,128)} fusion(f32[3,3,384,8,128]{4,2,0,1,3:T(8,128)S(1)} %get-tuple-element.138, f32[3,3,384,8,128]{4,2,0,1,3:T(8,128)S(1)} %get-tuple-element.137), kind=kLoop, calls=%fused_computation.48 | loop fusion | flops 4718592 | bytes 47185920 | tf_op jit(solution)/shard_map/add | solution.py:74
  538.7 6.2 slice_bitcast_fusion.27
  544.9 7.7 collective-permute-start.26
  556.5 6.6 collective-permute-start.28
  563.0 9.9 %slice_bitcast_fusion.3 = (f32[3,3,384,8,128]{4,2,0,1,3:T(8,128)S(1)}, f32[3,3,384,8,128]{4,2,0,1,3:T(8,128)S(1)}) fusion(f32[2,3,3,384,8,128]{5,3,1,2,4,0:T(8,128)} %bitcast.339), kind=kLoop, calls=%fused_computation.56 | loop fusion | bytes 56623104 | tf_op jit(solution)/shard_map/squeeze | solution.py:72
  573.0 7.7 pad_add_fusion.1
  583.6 4.1 copy-done.3
  587.8 6.1 slice_bitcast_fusion.9
  593.9 4.0 collective-permute-start.27
  603.6 5.7 slice_bitcast_fusion.33
  609.3 5.0 collective-permute-start.18
  614.3 6.2 slice_bitcast_fusion.11
  620.4 8.2 collective-permute-start.16
  633.5 22.0 %collective-permute-done.23 = bf16[384,8,128]{2,0,1:T(8,128)(2,1)S(1)} collective-permute-done((bf16[384,8,128]{2,0,1:T(8,128)(2,1)S(1)}, bf16[384,8,128]{2,0,1:T(8,128)(2,1)S(1)}, u32[]{:S(2)}, u32[]{:S(2)}) %collective-permute-start.23) | collective-permute-done | bytes 786464 | tf_op jit(solution)/shard_map/ppermute | solution.py:16
  663.6 64.1 %collective-permute-done.22 = bf16[384,8,128]{2,0,1:T(8,128)(2,1)S(1)} collective-permute-done((bf16[384,8,128]{2,0,1:T(8,128)(2,1)S(1)}, bf16[384,8,128]{2,0,1:T(8,128)(2,1)S(1)}, u32[]{:S(2)}, u32[]{:S(2)}) %collective-permute-start.22) | collective-permute-done | bytes 786464 | tf_op jit(solution)/shard_map/ppermute | solution.py:16
  729.0 18.3 %collective-permute-start.20 = (bf16[384,8,128]{2,0,1:T(8,128)(2,1)}, bf16[384,8,128]{2,0,1:T(8,128)(2,1)}, u32[]{:S(2)}, u32[]{:S(2)}) collective-permute-start(bf16[384,8,128]{2,0,1:T(8,128)(2,1)} %get-tuple-element.155), channel_id=1, source_target_pairs={{0,10},{2,12},{4,14},{6,16},{8,18},{10,20},{12,22},{14,24},{16,26}... | collective-permute-start | bytes 2359304 | tf_op jit(solution)/shard_map/ppermute | solution.py:16
  749.5 6.9 fusion.54
  759.6 3.7 all-to-all-start.6
  763.3 16.9 %collective-permute-done.19 = bf16[384,8,128]{2,0,1:T(8,128)(2,1)} collective-permute-done((bf16[384,8,128]{2,0,1:T(8,128)(2,1)}, bf16[384,8,128]{2,0,1:T(8,128)(2,1)}, u32[]{:S(2)}, u32[]{:S(2)}) %collective-permute-start.19) | collective-permute-done | bytes 786464 | tf_op jit(solution)/shard_map/ppermute | solution.py:16
  780.2 7.2 fusion.60
  794.7 4.6 all-to-all-start.5
  805.1 14.5 %all-to-all-done.5 = bf16[2,384,1024]{1,2,0:T(8,128)(2,1)} async-done(((bf16[2,384,1024]{1,2,0:T(8,128)(2,1)}), bf16[2,384,1024]{1,2,0:T(8,128)(2,1)}, u32[]{:S(2)}, u32[]{:S(2)}) %all-to-all-start.5) | async-done | bytes 1572896 | tf_op jit(solution)/shard_map/all_to_all | solution.py:203
  (261 shorter events, 332.2 us)
Async XLA Ops:
  0.6 69.7 %copy-start = (s32[16,2]{0,1:T(2,128)S(1)}, s32[16,2]{0,1:T(2,128)}, u32[]{:S(2)}) copy-start(s32[16,2]{0,1:T(2,128)} %param.11) | copy-start | bytes 388
  3.4 23.2 %all-to-all-start.2 = ((bf16[384,2,1024]{0,2,1:T(8,128)(2,1)}), bf16[384,2,1024]{0,2,1:T(8,128)(2,1)S(1)}, u32[]{:S(2)}, u32[]{:S(2)}) async-start(bf16[384,2,1024]{0,2,1:T(8,128)(2,1)} %bitcast.40), calls=%async_computation.2 | async-start | bytes 3145728 | tf_op jit(solution)/shard_map/all_to_all | solution.py:149
  26.5 22.3 %all-to-all-start = ((bf16[384,2,1024]{0,2,1:T(8,128)(2,1)}), bf16[384,2,1024]{0,2,1:T(8,128)(2,1)S(1)}, u32[]{:S(2)}, u32[]{:S(2)}) async-start(bf16[384,2,1024]{0,2,1:T(8,128)(2,1)} %bitcast.351), calls=%async_computation | async-start | bytes 3145728 | tf_op jit(solution)/shard_map/all_to_all | solution.py:148
  31.5 23.1 %collective-permute-start.12 = (bf16[384,8,128]{0,2,1:T(8,128)(2,1)}, bf16[384,8,128]{0,2,1:T(8,128)(2,1)}, u32[]{:S(2)}, u32[]{:S(2)}) collective-permute-start(bf16[384,8,128]{0,2,1:T(8,128)(2,1)} %bitcast.45), channel_id=1, source_target_pairs={{8,0},{10,2},{12,4},{14,6},{16,8},{18,10},{20,12},{22,14},{24,16},... | collective-permute-start | bytes 2359304 | tf_op jit(solution)/shard_map/ppermute | solution.py:16
  32.8 28.3 %collective-permute-start.11 = (bf16[384,8,128]{0,2,1:T(8,128)(2,1)}, bf16[384,8,128]{0,2,1:T(8,128)(2,1)}, u32[]{:S(2)}, u32[]{:S(2)}) collective-permute-start(bf16[384,8,128]{0,2,1:T(8,128)(2,1)} %bitcast.42), channel_id=1, source_target_pairs={{0,8},{2,10},{4,12},{6,14},{8,16},{10,18},{12,20},{14,22},{16,24},... | collective-permute-start | bytes 2359304 | tf_op jit(solution)/shard_map/ppermute | solution.py:16
  50.1 21.9 %collective-permute-start.7 = (bf16[384,8,128]{0,2,1:T(8,128)(2,1)}, bf16[384,8,128]{0,2,1:T(8,128)(2,1)}, u32[]{:S(2)}, u32[]{:S(2)}) collective-permute-start(bf16[384,8,128]{0,2,1:T(8,128)(2,1)} %bitcast.21), channel_id=1, source_target_pairs={{10,0},{12,2},{14,4},{16,6},{18,8},{20,10},{22,12},{24,14},{26,16}... | collective-permute-start | bytes 2359304 | tf_op jit(solution)/shard_map/ppermute | solution.py:16
  51.4 97.5 %collective-permute-start.6 = (bf16[2,384,8,128]{1,3,2,0:T(8,128)(2,1)S(1)}, bf16[2,384,8,128]{1,3,2,0:T(8,128)(2,1)}, u32[]{:S(2)}, u32[]{:S(2)}) collective-permute-start(bf16[2,384,8,128]{1,3,2,0:T(8,128)(2,1)S(1)} %bitcast.346), channel_id=1, source_target_pairs={{2,0},{4,2},{6,4},{8,6},{10,8},{12,10},{14,12},{16,14},{18,16},{20... | collective-permute-start | bytes 4718600 | tf_op jit(solution)/shard_map/ppermute | solution.py:16
  53.3 35.7 %collective-permute-start.4 = (bf16[384,8,128]{0,2,1:T(8,128)(2,1)}, bf16[384,8,128]{0,2,1:T(8,128)(2,1)}, u32[]{:S(2)}, u32[]{:S(2)}) collective-permute-start(bf16[384,8,128]{0,2,1:T(8,128)(2,1)} %bitcast.21), channel_id=1, source_target_pairs={{8,0},{10,2},{12,4},{14,6},{16,8},{18,10},{20,12},{22,14},{24,16},... | collective-permute-start | bytes 2359304 | tf_op jit(solution)/shard_map/ppermute | solution.py:16
  54.7 35.7 %collective-permute-start.3 = (bf16[384,8,128]{0,2,1:T(8,128)(2,1)}, bf16[384,8,128]{0,2,1:T(8,128)(2,1)}, u32[]{:S(2)}, u32[]{:S(2)}) collective-permute-start(bf16[384,8,128]{0,2,1:T(8,128)(2,1)} %bitcast.18), channel_id=1, source_target_pairs={{0,8},{2,10},{4,12},{6,14},{8,16},{10,18},{12,20},{14,22},{16,24},... | collective-permute-start | bytes 2359304 | tf_op jit(solution)/shard_map/ppermute | solution.py:16
  61.1 101.2 %collective-permute-start.1 = (bf16[2,384,8,128]{1,3,2,0:T(8,128)(2,1)S(1)}, bf16[2,384,8,128]{1,3,2,0:T(8,128)(2,1)}, u32[]{:S(2)}, u32[]{:S(2)}) collective-permute-start(bf16[2,384,8,128]{1,3,2,0:T(8,128)(2,1)S(1)} %bitcast.347), channel_id=1, source_target_pairs={{0,2},{2,4},{4,6},{6,8},{8,10},{10,12},{12,14},{14,16},{16,18},{18... | collective-permute-start | bytes 4718600 | tf_op jit(solution)/shard_map/ppermute | solution.py:16
  65.6 177.2 %all-to-all-start.1 = ((bf16[384,2,1024]{0,2,1:T(8,128)(2,1)}), bf16[384,2,1024]{0,2,1:T(8,128)(2,1)}, u32[]{:S(2)}, u32[]{:S(2)}) async-start(bf16[384,2,1024]{0,2,1:T(8,128)(2,1)} %bitcast.349), calls=%async_computation.1 | async-start | bytes 3145728 | tf_op jit(solution)/shard_map/all_to_all | solution.py:147
  72.0 75.6 %collective-permute-start.5 = (bf16[384,8,128]{0,2,1:T(8,128)(2,1)}, bf16[384,8,128]{0,2,1:T(8,128)(2,1)}, u32[]{:S(2)}, u32[]{:S(2)}) collective-permute-start(bf16[384,8,128]{0,2,1:T(8,128)(2,1)} %bitcast.18), channel_id=1, source_target_pairs={{0,6},{2,8},{4,10},{6,12},{8,14},{10,16},{12,18},{14,20},{16,22},{... | collective-permute-start | bytes 2359304 | tf_op jit(solution)/shard_map/ppermute | solution.py:16
  89.0 65.2 %collective-permute-start.2 = (bf16[384,8,128]{0,2,1:T(8,128)(2,1)}, bf16[384,8,128]{0,2,1:T(8,128)(2,1)}, u32[]{:S(2)}, u32[]{:S(2)}) collective-permute-start(bf16[384,8,128]{0,2,1:T(8,128)(2,1)} %bitcast.21), channel_id=1, source_target_pairs={{6,0},{8,2},{10,4},{12,6},{14,8},{16,10},{18,12},{20,14},{22,16},{... | collective-permute-start | bytes 2359304 | tf_op jit(solution)/shard_map/ppermute | solution.py:16
  90.3 70.0 %collective-permute-start = (bf16[384,8,128]{0,2,1:T(8,128)(2,1)}, bf16[384,8,128]{0,2,1:T(8,128)(2,1)}, u32[]{:S(2)}, u32[]{:S(2)}) collective-permute-start(bf16[384,8,128]{0,2,1:T(8,128)(2,1)} %bitcast.18), channel_id=1, source_target_pairs={{0,10},{2,12},{4,14},{6,16},{8,18},{10,20},{12,22},{14,24},{16,26}... | collective-permute-start | bytes 2359304 | tf_op jit(solution)/shard_map/ppermute | solution.py:16
  147.7 36.2 %collective-permute-start.15 = (bf16[384,8,128]{0,2,1:T(8,128)(2,1)}, bf16[384,8,128]{0,2,1:T(8,128)(2,1)}, u32[]{:S(2)}, u32[]{:S(2)}) collective-permute-start(bf16[384,8,128]{0,2,1:T(8,128)(2,1)} %bitcast.45), channel_id=1, source_target_pairs={{10,0},{12,2},{14,4},{16,6},{18,8},{20,10},{22,12},{24,14},{26,16}... | collective-permute-start | bytes 2359304 | tf_op jit(solution)/shard_map/ppermute | solution.py:16
  149.0 70.9 %collective-permute-start.10 = (bf16[384,8,128]{0,2,1:T(8,128)(2,1)}, bf16[384,8,128]{0,2,1:T(8,128)(2,1)}, u32[]{:S(2)}, u32[]{:S(2)}) collective-permute-start(bf16[384,8,128]{0,2,1:T(8,128)(2,1)} %bitcast.45), channel_id=1, source_target_pairs={{6,0},{8,2},{10,4},{12,6},{14,8},{16,10},{18,12},{20,14},{22,16},{... | collective-permute-start | bytes 2359304 | tf_op jit(solution)/shard_map/ppermute | solution.py:16
  154.3 61.7 %collective-permute-start.13 = (bf16[384,8,128]{0,2,1:T(8,128)(2,1)}, bf16[384,8,128]{0,2,1:T(8,128)(2,1)}, u32[]{:S(2)}, u32[]{:S(2)}) collective-permute-start(bf16[384,8,128]{0,2,1:T(8,128)(2,1)} %bitcast.42), channel_id=1, source_target_pairs={{0,6},{2,8},{4,10},{6,12},{8,14},{10,16},{12,18},{14,20},{16,22},{... | collective-permute-start | bytes 2359304 | tf_op jit(solution)/shard_map/ppermute | solution.py:16
  160.3 55.6 %collective-permute-start.14 = (bf16[2,384,8,128]{1,3,2,0:T(8,128)(2,1)S(1)}, bf16[2,384,8,128]{1,3,2,0:T(8,128)(2,1)}, u32[]{:S(2)}, u32[]{:S(2)}) collective-permute-start(bf16[2,384,8,128]{1,3,2,0:T(8,128)(2,1)S(1)} %bitcast.343), channel_id=1, source_target_pairs={{2,0},{4,2},{6,4},{8,6},{10,8},{12,10},{14,12},{16,14},{18,16},{20... | collective-permute-start | bytes 4718600 | tf_op jit(solution)/shard_map/ppermute | solution.py:16
  162.3 57.6 %collective-permute-start.9 = (bf16[2,384,8,128]{1,3,2,0:T(8,128)(2,1)S(1)}, bf16[2,384,8,128]{1,3,2,0:T(8,128)(2,1)S(1)}, u32[]{:S(2)}, u32[]{:S(2)}) collective-permute-start(bf16[2,384,8,128]{1,3,2,0:T(8,128)(2,1)S(1)} %bitcast.344), channel_id=1, source_target_pairs={{0,2},{2,4},{4,6},{6,8},{8,10},{10,12},{12,14},{14,16},{16,18},{18... | collective-permute-start | bytes 4718600 | tf_op jit(solution)/shard_map/ppermute | solution.py:16
  183.8 36.0 %collective-permute-start.8 = (bf16[384,8,128]{0,2,1:T(8,128)(2,1)}, bf16[384,8,128]{0,2,1:T(8,128)(2,1)}, u32[]{:S(2)}, u32[]{:S(2)}) collective-permute-start(bf16[384,8,128]{0,2,1:T(8,128)(2,1)} %bitcast.42), channel_id=1, source_target_pairs={{0,10},{2,12},{4,14},{6,16},{8,18},{10,20},{12,22},{14,24},{16,26}... | collective-permute-start | bytes 2359304 | tf_op jit(solution)/shard_map/ppermute | solution.py:16
  242.8 33.2 %all-to-all-start.3 = ((bf16[384,2,1024]{0,2,1:T(8,128)(2,1)}), bf16[384,2,1024]{0,2,1:T(8,128)(2,1)S(1)}, u32[]{:S(2)}, u32[]{:S(2)}) async-start(bf16[384,2,1024]{0,2,1:T(8,128)(2,1)} %bitcast.59), calls=%async_computation.3 | async-start | bytes 3145728 | tf_op jit(solution)/shard_map/all_to_all | solution.py:150
  257.2 18.8 %copy-start.8 = (bf16[16,384,128]{2,1,0:T(8,128)(2,1)S(1)}, bf16[16,384,128]{2,1,0:T(8,128)(2,1)}, u32[]{:S(2)}) copy-start(bf16[16,384,128]{2,1,0:T(8,128)(2,1)} %custom-call) | copy-start | bytes 4718596
  523.8 14.9 %copy-start.5 = (f32[3,3,384,8,128]{4,2,0,1,3:T(8,128)}, f32[3,3,384,8,128]{4,2,0,1,3:T(8,128)S(1)}, u32[]{:S(2)}) copy-start(f32[3,3,384,8,128]{4,2,0,1,3:T(8,128)S(1)} %get-tuple-element.138) | copy-start | bytes 42467332
  544.9 49.0 %collective-permute-start.26 = (bf16[384,8,128]{2,0,1:T(8,128)(2,1)}, bf16[384,8,128]{2,0,1:T(8,128)(2,1)}, u32[]{:S(2)}, u32[]{:S(2)}) collective-permute-start(bf16[384,8,128]{2,0,1:T(8,128)(2,1)} %get-tuple-element.145), channel_id=1, source_target_pairs={{0,6},{2,8},{4,10},{6,12},{8,14},{10,16},{12,18},{14,20},{16,22},{... | collective-permute-start | bytes 2359304 | tf_op jit(solution)/shard_map/ppermute | solution.py:16
  552.6 45.3 %collective-permute-start.31 = (bf16[384,8,128]{2,0,1:T(8,128)(2,1)}, bf16[384,8,128]{2,0,1:T(8,128)(2,1)}, u32[]{:S(2)}, u32[]{:S(2)}) collective-permute-start(bf16[384,8,128]{2,0,1:T(8,128)(2,1)} %get-tuple-element.146), channel_id=1, source_target_pairs={{6,0},{8,2},{10,4},{12,6},{14,8},{16,10},{18,12},{20,14},{22,16},{... | collective-permute-start | bytes 2359304 | tf_op jit(solution)/shard_map/ppermute | solution.py:16
  553.9 46.9 %collective-permute-start.30 = (bf16[384,8,128]{2,0,1:T(8,128)(2,1)}, bf16[384,8,128]{2,0,1:T(8,128)(2,1)}, u32[]{:S(2)}, u32[]{:S(2)}) collective-permute-start(bf16[384,8,128]{2,0,1:T(8,128)(2,1)} %get-tuple-element.147), channel_id=1, source_target_pairs={{8,0},{10,2},{12,4},{14,6},{16,8},{18,10},{20,12},{22,14},{24,16},... | collective-permute-start | bytes 2359304 | tf_op jit(solution)/shard_map/ppermute | solution.py:16
  555.2 54.1 %collective-permute-start.29 = (bf16[384,8,128]{2,0,1:T(8,128)(2,1)}, bf16[384,8,128]{2,0,1:T(8,128)(2,1)}, u32[]{:S(2)}, u32[]{:S(2)}) collective-permute-start(bf16[384,8,128]{2,0,1:T(8,128)(2,1)} %get-tuple-element.148), channel_id=1, source_target_pairs={{10,0},{12,2},{14,4},{16,6},{18,8},{20,10},{22,12},{24,14},{26,16}... | collective-permute-start | bytes 2359304 | tf_op jit(solution)/shard_map/ppermute | solution.py:16
  556.5 64.0 %collective-permute-start.28 = (bf16[384,8,128]{2,0,1:T(8,128)(2,1)}, bf16[384,8,128]{2,0,1:T(8,128)(2,1)}, u32[]{:S(2)}, u32[]{:S(2)}) collective-permute-start(bf16[384,8,128]{2,0,1:T(8,128)(2,1)} %get-tuple-element.149), channel_id=1, source_target_pairs={{0,10},{2,12},{4,14},{6,16},{8,18},{10,20},{12,22},{14,24},{16,26}... | collective-permute-start | bytes 2359304 | tf_op jit(solution)/shard_map/ppermute | solution.py:16
  573.0 14.8 %copy-start.3 = (f32[3,3,384,8,128]{4,2,0,1,3:T(8,128)}, f32[3,3,384,8,128]{4,2,0,1,3:T(8,128)S(1)}, u32[]{:S(2)}) copy-start(f32[3,3,384,8,128]{4,2,0,1,3:T(8,128)S(1)} %get-tuple-element.140) | copy-start | bytes 42467332
  593.9 34.7 %collective-permute-start.27 = (bf16[384,8,128]{2,0,1:T(8,128)(2,1)}, bf16[384,8,128]{2,0,1:T(8,128)(2,1)S(1)}, u32[]{:S(2)}, u32[]{:S(2)}) collective-permute-start(bf16[384,8,128]{2,0,1:T(8,128)(2,1)} %get-tuple-element.150), channel_id=1, source_target_pairs={{0,8},{2,10},{4,12},{6,14},{8,16},{10,18},{12,20},{14,22},{16,24},... | collective-permute-start | bytes 2359304 | tf_op jit(solution)/shard_map/ppermute | solution.py:16
  597.9 131.2 %collective-permute-start.24 = (f32[2,384,8,128]{3,1,2,0:T(8,128)}, f32[2,384,8,128]{3,1,2,0:T(8,128)}, u32[]{:S(2)}, u32[]{:S(2)}) collective-permute-start(f32[2,384,8,128]{3,1,2,0:T(8,128)} %get-tuple-element.141), channel_id=1, source_target_pairs={{2,0},{4,2},{6,4},{8,6},{10,8},{12,10},{14,12},{16,14},{18,16},{20... | collective-permute-start | bytes 9437192 | tf_op jit(solution)/shard_map/ppermute | solution.py:16
  600.8 146.5 %collective-permute-start.25 = (f32[2,384,8,128]{3,1,2,0:T(8,128)}, f32[2,384,8,128]{3,1,2,0:T(8,128)}, u32[]{:S(2)}, u32[]{:S(2)}) collective-permute-start(f32[2,384,8,128]{3,1,2,0:T(8,128)} %get-tuple-element.142), channel_id=1, source_target_pairs={{0,2},{2,4},{4,6},{6,8},{8,10},{10,12},{12,14},{14,16},{16,18},{18... | collective-permute-start | bytes 9437192 | tf_op jit(solution)/shard_map/ppermute | solution.py:16
  609.3 47.6 %copy-start.10 = (bf16[16,384,128]{2,1,0:T(8,128)(2,1)S(1)}, bf16[16,384,128]{2,1,0:T(8,128)(2,1)}, u32[]{:S(2)}) copy-start(bf16[16,384,128]{2,1,0:T(8,128)(2,1)} %copy-done.9) | copy-start | bytes 4718596
  609.3 22.9 %collective-permute-start.18 = (bf16[384,8,128]{2,0,1:T(8,128)(2,1)S(1)}, bf16[384,8,128]{2,0,1:T(8,128)(2,1)S(1)}, u32[]{:S(2)}, u32[]{:S(2)}) collective-permute-start(bf16[384,8,128]{2,0,1:T(8,128)(2,1)S(1)} %get-tuple-element.151), channel_id=1, source_target_pairs={{0,6},{2,8},{4,10},{6,12},{8,14},{10,16},{12,18},{14,20},{16,22},{... | collective-permute-start | bytes 2359304 | tf_op jit(solution)/shard_map/ppermute | solution.py:16
  620.4 159.7 %collective-permute-start.16 = (f32[2,384,8,128]{3,1,2,0:T(8,128)}, f32[2,384,8,128]{3,1,2,0:T(8,128)}, u32[]{:S(2)}, u32[]{:S(2)}) collective-permute-start(f32[2,384,8,128]{3,1,2,0:T(8,128)} %get-tuple-element.143), channel_id=1, source_target_pairs={{2,0},{4,2},{6,4},{8,6},{10,8},{12,10},{14,12},{16,14},{18,16},{20... | collective-permute-start | bytes 9437192 | tf_op jit(solution)/shard_map/ppermute | solution.py:16
  628.6 29.3 %copy-start.13 = (bf16[384,8,128]{2,0,1:T(8,128)(2,1)}, bf16[384,8,128]{2,0,1:T(8,128)(2,1)S(1)}, u32[]{:S(2)}) copy-start(bf16[384,8,128]{2,0,1:T(8,128)(2,1)S(1)} %collective-permute-done.27) | copy-start | bytes 2359300
  628.6 151.6 %collective-permute-start.17 = (f32[2,384,8,128]{3,1,2,0:T(8,128)}, f32[2,384,8,128]{3,1,2,0:T(8,128)}, u32[]{:S(2)}, u32[]{:S(2)}) collective-permute-start(f32[2,384,8,128]{3,1,2,0:T(8,128)} %get-tuple-element.144), channel_id=1, source_target_pairs={{0,2},{2,4},{4,6},{6,8},{8,10},{10,12},{12,14},{14,16},{16,18},{18... | collective-permute-start | bytes 9437192 | tf_op jit(solution)/shard_map/ppermute | solution.py:16
  632.2 25.7 %copy-start.12 = (bf16[384,8,128]{2,0,1:T(8,128)(2,1)}, bf16[384,8,128]{2,0,1:T(8,128)(2,1)S(1)}, u32[]{:S(2)}) copy-start(bf16[384,8,128]{2,0,1:T(8,128)(2,1)S(1)} %collective-permute-done.18) | copy-start | bytes 2359300
  632.2 23.3 %collective-permute-start.23 = (bf16[384,8,128]{2,0,1:T(8,128)(2,1)S(1)}, bf16[384,8,128]{2,0,1:T(8,128)(2,1)S(1)}, u32[]{:S(2)}, u32[]{:S(2)}) collective-permute-start(bf16[384,8,128]{2,0,1:T(8,128)(2,1)S(1)} %get-tuple-element.152), channel_id=1, source_target_pairs={{6,0},{8,2},{10,4},{12,6},{14,8},{16,10},{18,12},{20,14},{22,16},{... | collective-permute-start | bytes 2359304 | tf_op jit(solution)/shard_map/ppermute | solution.py:16
  655.5 72.2 %collective-permute-start.22 = (bf16[384,8,128]{2,0,1:T(8,128)(2,1)S(1)}, bf16[384,8,128]{2,0,1:T(8,128)(2,1)S(1)}, u32[]{:S(2)}, u32[]{:S(2)}) collective-permute-start(bf16[384,8,128]{2,0,1:T(8,128)(2,1)S(1)} %get-tuple-element.153), channel_id=1, source_target_pairs={{8,0},{10,2},{12,4},{14,6},{16,8},{18,10},{20,12},{22,14},{24,16},... | collective-permute-start | bytes 2359304 | tf_op jit(solution)/shard_map/ppermute | solution.py:16
  660.0 99.6 %all-to-all-start.4 = ((bf16[2,384,1024]{2,1,0:T(8,128)(2,1)}), bf16[2,384,1024]{2,1,0:T(8,128)(2,1)S(1)}, u32[]{:S(2)}, u32[]{:S(2)}) async-start(bf16[2,384,1024]{2,1,0:T(8,128)(2,1)} %convert_element_type.116), calls=%async_computation.4 | async-start | bytes 3145728 | tf_op jit(solution)/shard_map/all_to_all | solution.py:202
  727.7 19.6 %copy-start.15 = (bf16[384,8,128]{2,0,1:T(8,128)(2,1)}, bf16[384,8,128]{2,0,1:T(8,128)(2,1)S(1)}, u32[]{:S(2)}) copy-start(bf16[384,8,128]{2,0,1:T(8,128)(2,1)S(1)} %collective-permute-done.22) | copy-start | bytes 2359300
  727.7 35.6 %collective-permute-start.21 = (bf16[384,8,128]{2,0,1:T(8,128)(2,1)}, bf16[384,8,128]{2,0,1:T(8,128)(2,1)}, u32[]{:S(2)}, u32[]{:S(2)}) collective-permute-start(bf16[384,8,128]{2,0,1:T(8,128)(2,1)} %get-tuple-element.154), channel_id=1, source_target_pairs={{10,0},{12,2},{14,4},{16,6},{18,8},{20,10},{22,12},{24,14},{26,16}... | collective-permute-start | bytes 2359304 | tf_op jit(solution)/shard_map/ppermute | solution.py:16
  729.0 34.3 %collective-permute-start.20 = (bf16[384,8,128]{2,0,1:T(8,128)(2,1)}, bf16[384,8,128]{2,0,1:T(8,128)(2,1)}, u32[]{:S(2)}, u32[]{:S(2)}) collective-permute-start(bf16[384,8,128]{2,0,1:T(8,128)(2,1)} %get-tuple-element.155), channel_id=1, source_target_pairs={{0,10},{2,12},{4,14},{6,16},{8,18},{10,20},{12,22},{14,24},{16,26}... | collective-permute-start | bytes 2359304 | tf_op jit(solution)/shard_map/ppermute | solution.py:16
  747.3 32.9 %collective-permute-start.19 = (bf16[384,8,128]{2,0,1:T(8,128)(2,1)}, bf16[384,8,128]{2,0,1:T(8,128)(2,1)}, u32[]{:S(2)}, u32[]{:S(2)}) collective-permute-start(bf16[384,8,128]{2,0,1:T(8,128)(2,1)} %get-tuple-element.156), channel_id=1, source_target_pairs={{0,8},{2,10},{4,12},{6,14},{8,16},{10,18},{12,20},{14,22},{16,24},... | collective-permute-start | bytes 2359304 | tf_op jit(solution)/shard_map/ppermute | solution.py:16
  759.6 35.1 %all-to-all-start.6 = ((bf16[2,384,1024]{1,2,0:T(8,128)(2,1)}), bf16[2,384,1024]{1,2,0:T(8,128)(2,1)S(1)}, u32[]{:S(2)}, u32[]{:S(2)}) async-start(bf16[2,384,1024]{1,2,0:T(8,128)(2,1)} %pad_maximum_fusion.3), calls=%async_computation.6 | async-start | bytes 3145728 | tf_op jit(solution)/shard_map/all_to_all | solution.py:204
  794.7 25.0 %all-to-all-start.5 = ((bf16[2,384,1024]{1,2,0:T(8,128)(2,1)}), bf16[2,384,1024]{1,2,0:T(8,128)(2,1)}, u32[]{:S(2)}, u32[]{:S(2)}) async-start(bf16[2,384,1024]{1,2,0:T(8,128)(2,1)} %pad_maximum_fusion.2), calls=%async_computation.5 | async-start | bytes 3145728 | tf_op jit(solution)/shard_map/all_to_all | solution.py:203
  803.5 18.7 %copy-start.1 = (s32[16,2]{0,1:T(2,128)S(1)}, s32[16,2]{0,1:T(2,128)}, u32[]{:S(2)}) copy-start(s32[16,2]{0,1:T(2,128)} %param.11) | copy-start | bytes 388
  (7 other events, 30.7 us)
where the time goes:
time: 833 us; the launch traced here: 822 us
  matrix products  194 us (23%)
  starting transfers between devices  191 us (23%)
  waiting for transfers between devices  159 us (19%)
  local copies, waits for them, and re-layouts  145 us (17%)
  other arithmetic  132 us (16%)
    ppermute x32, starting transfers between devices, passed_along(): return lax.ppermute(block, axis, route)  163 us
    ppermute x32, waiting for transfers between devices, passed_along(): return lax.ppermute(block, axis, route)  116 us
    dot_general x16, matrix products, query_with_terms(): jnp.einsum('oqk,qd->okd', dscore, query_head, preferred_element_type=jnp....  47.8 us
    dot_general x16, matrix products, query_core(): jnp.einsum('qd,okd->oqk', grad_head, value_head, preferred_element_type=j...  41 us
    dot_general x16, matrix products, query_with_terms(): jnp.einsum('oqk,qd->okd', rounded_probs, grad_head, preferred_element_typ...  39.1 us
    another operation x8, other arithmetic, neighbour_columns(): jnp.stack([column[member_num] for column in columns])  38.4 us
    transpose x2, local copies, waits for them, and re-layouts, column_windows(): picked = jnp.transpose(picked, (0, 4, 2, 1, 3, 5))  37.4 us
    dot_general x16, matrix products, query_core(): jnp.einsum('oqk,okd->qd', dscore, key_head, preferred_element_type=jnp.fl...  33.6 us
  transfers between devices with their start and end apart: 39, of which 9 were waited for; matrix products, arithmetic and copies ran while one was open for 23% of the time, Pallas kernels for 0%

commit v1 on v0

v1 whole, which is shorter than its diff:
```python
import functools

import jax
import jax.numpy as jnp
from jax import lax
from jax.experimental import pallas as pl
from jax.experimental.pallas import tpu as pltpu
from jax.sharding import PartitionSpec as P

HD = 128
GH = 4
SCALE = HD ** (-0.5)
LOG2E = 1.4426950408889634


def passed_along(block, axis, distance):
    devices = range(lax.axis_size(axis))
    route = [(i - distance, i) for i in devices if i - distance in devices]
    return lax.ppermute(block, axis, route)


def visible_slots(window, heads_here):
    seq_index = lax.axis_index("seq")
    grid_time = 2 * (lax.axis_size("seq") // GH)
    reaches = lax.dynamic_slice_in_dim(window, lax.axis_index("head") * heads_here, heads_here, 0)
    slot = jnp.arange(9)
    time_off, row_off = slot // 3 - 1, slot % 3 - 1
    near_time = 2 * (seq_index // GH) + jnp.arange(2)[:, None] + time_off[None, :]
    near_row = seq_index % GH + row_off
    inside = (near_time >= 0) & (near_time < grid_time)
    inside = inside & ((near_row >= 0) & (near_row < GH))[None, :]
    reach = (jnp.abs(time_off)[None, :] <= reaches[:, :1]) & (
        jnp.abs(row_off)[None, :] <= reaches[:, 1:]
    )
    return (inside[None] & reach[:, None, :]).astype(jnp.int32).reshape(-1)


def dot(a, b, dims):
    return lax.dot_general(a, b, (dims, ((), ())), preferred_element_type=jnp.float32)


def attend_kernel(
    vis_ref, q_ref, g_ref, kv_ref, dq_ref, dkv_ref, e_scr, dp_scr, acc, dqt, top, total, delta
):
    head = pl.program_id(0)
    tile = q_ref.shape[1] // 2
    acc[...] = jnp.zeros_like(acc)

    def one_tile(qt, carry):
        rows = pl.ds(pl.multiple_of(qt * tile, tile), tile)
        q = q_ref[0, rows, :]
        g = g_ref[0, rows, :]
        top[...] = jnp.full_like(top, -jnp.inf)
        total[...] = jnp.zeros_like(total)
        delta[...] = jnp.zeros_like(delta)
        dqt[...] = jnp.zeros_like(dqt)

        def over_visible(body):
            def step(slot, carry):
                @pl.when(vis_ref[(head * 2 + qt) * 9 + slot] == 1)
                def _():
                    body(slot, lax.rem(slot, 3), qt + lax.div(slot, 3))

                return carry

            lax.fori_loop(0, 9, step, 0)

        def scores(slot, row, time):
            s = dot(kv_ref[0, 0, row, time], q, ((1,), (1,)))
            top[...] = jnp.maximum(top[...], jnp.max(s, axis=0, keepdims=True))
            e_scr[slot] = s
            dp_scr[slot] = dot(kv_ref[0, 1, row, time], g, ((1,), (1,)))

        def sums(slot, row, time):
            e = jnp.exp2((e_scr[slot] - top[...]) * (SCALE * LOG2E))
            e_scr[slot] = e
            total[...] += jnp.sum(e, axis=0, keepdims=True)
            delta[...] += jnp.sum(e * dp_scr[slot], axis=0, keepdims=True)

        def grads(slot, row, time):
            p = e_scr[slot] * total[...]
            ds = (p * (dp_scr[slot] - delta[...])).astype(jnp.bfloat16)
            acc[1, row, time] += dot(p.astype(jnp.bfloat16), g, ((1,), (0,)))
            acc[0, row, time] += dot(ds, q, ((1,), (0,)))
            dqt[...] += dot(kv_ref[0, 0, row, time], ds, ((0,), (0,)))

        over_visible(scores)
        over_visible(sums)
        total[...] = 1.0 / total[...]
        delta[...] = delta[...] * total[...]
        over_visible(grads)
        dq_ref[0, rows, :] = (dqt[...] * SCALE).T.astype(jnp.bfloat16)
        return carry

    lax.fori_loop(0, 2, one_tile, 0)
    dkv_ref[0, 0] = (acc[0] * SCALE).astype(jnp.bfloat16)
    dkv_ref[0, 1] = acc[1].astype(jnp.bfloat16)


def attend(vis, q, g, kv):
    heads, rows, _ = q.shape
    tile = rows // 2
    by_head = lambda shape: pl.BlockSpec(
        (1,) + shape, lambda n, vis: (n,) + (0,) * len(shape)
    )
    pairs = heads * 18
    return pl.pallas_call(
        attend_kernel,
        grid_spec=pltpu.PrefetchScalarGridSpec(
            num_scalar_prefetch=1,
            grid=(heads,),
            in_specs=[
                by_head((rows, HD)),
                by_head((rows, HD)),
                by_head((2, 3, 4, tile, HD)),
            ],
            out_specs=[by_head((rows, HD)), by_head((2, 3, 4, tile, HD))],
            scratch_shapes=[
                pltpu.VMEM((9, tile, tile), jnp.float32),
                pltpu.VMEM((9, tile, tile), jnp.float32),
                pltpu.VMEM((2, 3, 4, tile, HD), jnp.float32),
                pltpu.VMEM((HD, tile), jnp.float32),
                pltpu.VMEM((1, tile), jnp.float32),
                pltpu.VMEM((1, tile), jnp.float32),
                pltpu.VMEM((1, tile), jnp.float32),
            ],
        ),
        out_shape=[
            jax.ShapeDtypeStruct(q.shape, jnp.bfloat16),
            jax.ShapeDtypeStruct(kv.shape, jnp.bfloat16),
        ],
        compiler_params=pltpu.CompilerParams(
            dimension_semantics=("arbitrary",), vmem_limit_bytes=48 * 2**20
        ),
        cost_estimate=pl.CostEstimate(
            flops=pairs * 5 * tile * tile * HD,
            bytes_accessed=4 * kv.size + 6 * q.size,
            transcendentals=pairs * tile * tile // 2,
        ),
        name="attend",
    )(vis, q, g, kv)


def exchange_in(queries, keys, values, out_grad):
    packed = jnp.stack([queries, keys, values, out_grad])
    here = lax.all_to_all(packed, "head", split_axis=2, concat_axis=1, tiled=True)
    rows, heads = here.shape[1], here.shape[2] // HD
    here = jnp.transpose(here.reshape(4, rows, heads, HD), (2, 0, 1, 3))
    kv = here[:, 1:3].reshape(heads, 2, 2, rows // 2, HD)
    before = passed_along(kv[:, :, 1], "seq", GH)
    after = passed_along(kv[:, :, 0], "seq", -GH)
    column = jnp.concatenate([before[:, :, None], kv, after[:, :, None]], axis=2)
    kv = jnp.stack(
        [passed_along(column, "seq", 1), column, passed_along(column, "seq", -1)], axis=2
    )
    return here[:, 0], here[:, 3], kv


def exchange_out(dq, dkv):
    column = dkv[:, :, 1].astype(jnp.float32)
    column += passed_along(dkv[:, :, 0], "seq", -1).astype(jnp.float32)
    column += passed_along(dkv[:, :, 2], "seq", 1).astype(jnp.float32)
    edges = column.astype(jnp.bfloat16)
    first = column[:, :, 1] + passed_along(edges[:, :, 3], "seq", GH).astype(jnp.float32)
    second = column[:, :, 2] + passed_along(edges[:, :, 0], "seq", -GH).astype(jnp.float32)
    own = jnp.concatenate([first, second], axis=2).astype(jnp.bfloat16)
    packed = jnp.concatenate([dq[:, None], own], axis=1)
    heads, _, rows, _ = packed.shape
    packed = jnp.transpose(packed, (1, 2, 0, 3)).reshape(3, rows, heads * HD)
    return tuple(lax.all_to_all(packed, "head", split_axis=1, concat_axis=2, tiled=True))


def per_device(queries, keys, values, out_grad, window):
    q, g, kv = exchange_in(queries, keys, values, out_grad)
    dq, dkv = attend(visible_slots(window, q.shape[0]), q, g, kv)
    return exchange_out(dq, dkv)


def solution(mesh):
    rows = P(("seq", "head"), None)
    return jax.shard_map(
        per_device,
        mesh=mesh,
        in_specs=(rows, rows, rows, rows, P()),
        out_specs=(rows, rows, rows),
        check_vma=False,
    )
```

time: 833 us -> 644 us (0.77); the launches traced: 822 us -> 643 us
  matrix products: 194 us -> 0 us
  blocking collectives: 0 us -> 130 us
  starting transfers between devices: 191 us -> 87.4 us
  other arithmetic: 132 us -> 36.3 us
  waiting for transfers between devices: 159 us -> 254 us
  local copies, waits for them, and re-layouts: 145 us -> 76.5 us
  Pallas kernels: 0 us -> 57.7 us
    dot_general x80 -> x0, matrix products: 194 us -> none  [the longest x16 47.8 us: query_with_terms(): jnp.einsum('oqk,qd->okd', dscore, query_head, preferred_element_type=jnp....]
    ppermute x32 -> x8, waiting for transfers between devices: 116 us -> 254 us  [passed_along(): return lax.ppermute(block, axis, route)]
    all_to_all x0 -> x2, blocking collectives: none -> 130 us  [the longest x1 79.4 us: exchange_in(): lax.all_to_all(packed, 'head', split_axis=2, concat_axis=1, tiled=True)]
    ppermute x32 -> x8, starting transfers between devices: 163 us -> 87.4 us  [passed_along(): return lax.ppermute(block, axis, route)]
    pallas_call x0 -> x1, Pallas kernels: none -> 57.7 us  [attend(): pl.pallas_call(attend_kernel, grid_spec=pltpu.PrefetchScalarGridSpec(num_...]
    all_to_all x7 -> x0, waiting for transfers between devices: 43 us -> none  [the longest x1 17.9 us: per_device(): lax.all_to_all(values, 'head', split_axis=1, concat_axis=0, tiled=True)]
    another operation x14 -> x5, other arithmetic: 56.6 us -> 25.4 us  [the longest x2 18.1 us: exchange_in(): jnp.stack([passed_along(column, 'seq', 1), column, passed_along(column, '...]
    transpose x2 -> x1, local copies, waits for them, and re-layouts: 37.4 us -> 6.7 us  [exchange_out(): packed = jnp.transpose(packed, (1, 2, 0, 3)).reshape(3, rows, heads * HD)]
  transfers between devices with their start and end apart: 39 -> 8, of which waited for: 9 -> 8; matrix products, arithmetic and copies ran while one was open for 23% -> 1% of each run, Pallas kernels for 0% -> 0%
where the time goes in v1:
time: 644 us; the launch traced here: 643 us
  waiting for transfers between devices  254 us (39%)
  blocking collectives  130 us (20%)
  starting transfers between devices  87.4 us (14%)
  local copies, waits for them, and re-layouts  76.5 us (12%)
  Pallas kernels  57.7 us (9%)
  other arithmetic  36.3 us (6%)
    ppermute x8, waiting for transfers between devices, passed_along(): return lax.ppermute(block, axis, route)  254 us
    ppermute x8, starting transfers between devices, passed_along(): return lax.ppermute(block, axis, route)  87.4 us
    all_to_all x1, blocking collectives, exchange_in(): lax.all_to_all(packed, 'head', split_axis=2, concat_axis=1, tiled=True)  79.4 us
    pallas_call x1, Pallas kernels, attend(): pl.pallas_call(attend_kernel, grid_spec=pltpu.PrefetchScalarGridSpec(num_...  57.7 us
    all_to_all x1, blocking collectives, exchange_out(): lax.all_to_all(packed, 'head', split_axis=1, concat_axis=2, tiled=True)  50.4 us
    another operation x2, other arithmetic, exchange_in(): jnp.stack([passed_along(column, 'seq', 1), column, passed_along(column, '...  18.1 us
    unnamed x16, local copies, waits for them, and re-layouts  16.1 us
  transfers between devices with their start and end apart: 8, of which 8 were waited for; matrix products, arithmetic and copies ran while one was open for 1% of the time, Pallas kernels for 0%

profile of v1, /device:TPU:2, one launch (start us, length us, event | category | flops | bytes accessed | tf_op | source)
XLA Modules:
  0.0 642.7 jit_solution(18070175799489231632)
XLA Ops:
  0.6 6.5 %pad_maximum_fusion.1 = bf16[4,384,2048]{2,1,0:T(8,128)(2,1)} fusion(bf16[1,384,2048]{2,1,0:T(8,128)(2,1)} %bitcast.88, bf16[1,384,2048]{2,1,0:T(8,128)(2,1)} %bitcast.89, bf16[1,384,2048]{2,1,0:T(8,128)(2,1)} %bitcast.90, bf16[1,384,2048]{2,1,0:T(8,128)(2,1)} %bitcast.91), kind=kLoop, calls=%fused_computation.5 | loop fusion | flops 9437184 | bytes 12582912 | tf_op jit(solution)/shard_map/stack | solution.py:145
  7.1 10.7 %copy.72 = bf16[4,384,2048]{1,0,2:T(4,128)(2,1)} copy(bf16[4,384,2048]{2,1,0:T(8,128)(2,1)} %pad_maximum_fusion.1) | data formatting | bytes 12582912 | tf_op jit(solution)/shard_map/stack | solution.py:145
  17.9 79.4 %all_to_all.30 = bf16[4,384,2048]{1,0,2:T(4,128)(2,1)} all-to-all(bf16[4,384,2048]{1,0,2:T(4,128)(2,1)} %copy.72), channel_id=1, replica_groups=mesh['seq'=16,'head'=2] {'head'}, dimensions={2} | all-to-all | bytes 12582912 | tf_op jit(solution)/shard_map/all_to_all | solution.py:146
  97.2 10.6 %copy.73 = bf16[4,384,2,1024]{3,1,2,0:T(8,128)(2,1)} copy(bf16[4,384,2,1024]{1,0,3,2:T(4,128)(2,1)} %bitcast.79) | data formatting | bytes 12582912 | tf_op jit(solution)/shard_map/all_to_all | solution.py:146
  107.8 4.4 copy.96
  112.3 1.5 copy.110
  114.0 0.3 fusion.11
  114.3 2.1 copy-done.2
  116.7 1.3 collective-permute-start.1
  118.0 4.6 collective-permute-start
  122.6 0.3 copy.75
  122.9 30.9 %collective-permute-done.1 = bf16[8,2,384,128]{3,2,1,0:T(8,128)(2,1)S(1)} collective-permute-done((bf16[8,2,384,128]{3,2,1,0:T(8,128)(2,1)S(1)}, bf16[8,2,384,128]{3,2,1,0:T(8,128)(2,1)S(1)}, u32[]{:S(2)}, u32[]{:S(2)}) %collective-permute-start.1) | collective-permute-done | bytes 1572896 | tf_op jit(solution)/shard_map/ppermute | solution.py:19
  153.8 1.2 collective-permute-done
  155.0 5.0 fusion.9
  159.9 1.9 collective-permute-start.3
  161.9 2.4 collective-permute-start.2
  164.7 2.3 slice_bitcast_fusion.7
  167.1 63.6 %collective-permute-done.3 = bf16[8,2,4,384,128]{4,3,2,1,0:T(8,128)(2,1)} collective-permute-done((bf16[8,2,4,384,128]{4,3,2,1,0:T(8,128)(2,1)}, bf16[8,2,4,384,128]{4,3,2,1,0:T(8,128)(2,1)}, u32[]{:S(2)}, u32[]{:S(2)}) %collective-permute-start.3) | collective-permute-done | bytes 6291488 | tf_op jit(solution)/shard_map/ppermute | solution.py:19
  230.6 70.4 %collective-permute-done.2 = bf16[8,2,4,384,128]{4,3,2,1,0:T(8,128)(2,1)} collective-permute-done((bf16[8,2,4,384,128]{4,3,2,1,0:T(8,128)(2,1)}, bf16[8,2,4,384,128]{4,3,2,1,0:T(8,128)(2,1)}, u32[]{:S(2)}, u32[]{:S(2)}) %collective-permute-start.2) | collective-permute-done | bytes 6291488 | tf_op jit(solution)/shard_map/ppermute | solution.py:19
  301.1 13.1 %pad_maximum_fusion.kv_ref = bf16[8,2,3,4,384,128]{5,4,3,2,1,0:T(8,128)(2,1)} fusion(bf16[8,2,1,4,384,128]{5,4,3,2,1,0:T(8,128)(2,1)} %bitcast.21, bf16[8,2,1,4,384,128]{5,4,3,2,1,0:T(8,128)(2,1)S(1)} %copy-done.3, bf16[8,2,1,4,384,128]{5,4,3,2,1,0:T(8,128)(2,1)} %bitcast.18), kind=kLoop, calls=%fused_computation | loop fusion | flops 18874368 | bytes 37748736 | tf_op jit(solution)/shard_map/stack | solution.py:153
  314.2 57.7 %attend.1 = (bf16[8,768,128]{2,1,0:T(8,128)(2,1)S(1)}, bf16[8,2,3,4,384,128]{5,4,3,2,1,0:T(8,128)(2,1)}) custom-call(s32[144]{0:T(256)S(1)} %reshape.163.vis_ref, bf16[8,768,128]{2,1,0:T(8,128)(2,1)S(1)} %get-tuple-element.21.q_ref, bf16[8,768,128]{2,1,0:T(8,128)(2,1)S(1)} %get-tuple-element.20.g_ref, bf16[8,2,3,4,384,128]{5,4,3,2,1,0:T(8,128)(2,1)} %pad_maximum_fusion.kv_ref), custom_call_target="tpu_custom_call" | custom-call | flops 13589544960 | bytes 42467328 | tf_op jit(solution)/shard_map/attend/pallas_call | solution.py:107
  371.9 3.5 slice_bitcast_fusion.2
  375.4 3.5 slice_bitcast_fusion
  378.9 1.9 collective-permute-start.4
  380.9 2.4 collective-permute-start.5
  383.3 66.1 %collective-permute-done.4 = bf16[8,2,4,384,128]{4,3,2,1,0:T(8,128)(2,1)S(1)} collective-permute-done((bf16[8,2,4,384,128]{4,3,2,1,0:T(8,128)(2,1)S(1)}, bf16[8,2,4,384,128]{4,3,2,1,0:T(8,128)(2,1)S(1)}, u32[]{:S(2)}, u32[]{:S(2)}) %collective-permute-start.4) | collective-permute-done | bytes 6291488 | tf_op jit(solution)/shard_map/ppermute | solution.py:19
  449.3 2.6 copy-done.4
  451.9 1.3 collective-permute-done.5
  453.3 8.3 %fusion = f32[8,2,4,384,128]{4,3,2,1,0:T(8,128)S(1)} fusion(bf16[8,2,4,384,128]{4,3,2,1,0:T(8,128)(2,1)} %collective-permute-done.5, bf16[8,2,4,384,128]{4,3,2,1,0:T(8,128)(2,1)} %copy-done.4, bf16[8,2,3,4,384,128]{5,4,3,2,1,0:T(8,128)(2,1)} %get-tuple-element.6), kind=kLoop, calls=%fused_computation.2 | loop fusion | flops 15728640 | bytes 31457280 | tf_op jit(solution)/shard_map/add | solution.py:162
  461.6 0.5 slice_bitcast_fusion.6
  462.1 71.3 %collective-permute-start.6 = (bf16[8,2,384,128]{3,2,1,0:T(8,128)(2,1)S(1)}, bf16[8,2,384,128]{3,2,1,0:T(8,128)(2,1)S(1)}, u32[]{:S(2)}, u32[]{:S(2)}) collective-permute-start(bf16[8,2,384,128]{3,2,1,0:T(8,128)(2,1)S(1)} %get-tuple-element.16), channel_id=1, source_target_pairs={{0,8},{2,10},{4,12},{6,14},{8,16},{10,18},{12,20},{14,22},{16,24},... | collective-permute-start | bytes 4718600 | tf_op jit(solution)/shard_map/ppermute | solution.py:19
  533.4 1.5 collective-permute-start.7
  534.9 16.3 %collective-permute-done.6 = bf16[8,2,384,128]{3,2,1,0:T(8,128)(2,1)S(1)} collective-permute-done((bf16[8,2,384,128]{3,2,1,0:T(8,128)(2,1)S(1)}, bf16[8,2,384,128]{3,2,1,0:T(8,128)(2,1)S(1)}, u32[]{:S(2)}, u32[]{:S(2)}) %collective-permute-start.6) | collective-permute-done | bytes 1572896 | tf_op jit(solution)/shard_map/ppermute | solution.py:19
  551.2 0.4 fusion.4
  551.6 4.4 collective-permute-done.7
  556.0 0.4 fusion.2
  556.5 2.3 maximum_bitcast_fusion
  558.8 6.7 %copy.84 = bf16[3,768,8,128]{1,3,2,0:T(8,128)(2,1)} copy(bf16[3,768,8,128]{3,1,0,2:T(8,128)(2,1)} %maximum_bitcast_fusion) | data formatting | bytes 9437184 | tf_op jit(solution)/shard_map/transpose | solution.py:169
  565.5 11.0 %copy.85 = bf16[3,768,1024]{2,0,1:T(4,128)(2,1)} copy(bf16[3,768,1024]{1,2,0:T(8,128)(2,1)} %bitcast.83) | data formatting | bytes 9437184 | tf_op jit(solution)/shard_map/reshape | solution.py:169
  576.5 50.4 %all_to_all.31 = bf16[3,768,1024]{2,0,1:T(4,128)(2,1)S(1)} all-to-all(bf16[3,768,1024]{2,0,1:T(4,128)(2,1)} %copy.85), channel_id=1, replica_groups=mesh['seq'=16,'head'=2] {'head'}, dimensions={1} | all-to-all | bytes 9437184 | tf_op jit(solution)/shard_map/all_to_all | solution.py:170
  627.0 1.9 copy.86
  628.9 2.0 fusion.10
  630.9 2.6 copy.89
  633.4 2.6 copy.92
  636.0 1.6 copy.88
  637.6 2.6 copy.91
  640.2 0.9 copy.87
  641.0 1.6 copy.90
  (21 shorter events, 0.8 us)
Async XLA Ops:
  0.6 163.7 %copy-start = (s32[16,2]{0,1:T(2,128)S(1)}, s32[16,2]{0,1:T(2,128)}, u32[]{:S(2)}) copy-start(s32[16,2]{0,1:T(2,128)} %param.9) | copy-start | bytes 388
  113.7 2.7 copy-start.2
  116.7 37.2 %collective-permute-start.1 = (bf16[8,2,384,128]{3,2,1,0:T(8,128)(2,1)S(1)}, bf16[8,2,384,128]{3,2,1,0:T(8,128)(2,1)S(1)}, u32[]{:S(2)}, u32[]{:S(2)}) collective-permute-start(bf16[8,2,384,128]{3,2,1,0:T(8,128)(2,1)S(1)} %bitcast.95), channel_id=1, source_target_pairs={{8,0},{10,2},{12,4},{14,6},{16,8},{18,10},{20,12},{22,14},{24,16},... | collective-permute-start | bytes 4718600 | tf_op jit(solution)/shard_map/ppermute | solution.py:19
  118.0 37.0 %collective-permute-start = (bf16[8,2,384,128]{3,2,1,0:T(8,128)(2,1)S(1)}, bf16[8,2,384,128]{3,2,1,0:T(8,128)(2,1)S(1)}, u32[]{:S(2)}, u32[]{:S(2)}) collective-permute-start(bf16[8,2,384,128]{3,2,1,0:T(8,128)(2,1)S(1)} %bitcast.94), channel_id=1, source_target_pairs={{0,8},{2,10},{4,12},{6,14},{8,16},{10,18},{12,20},{14,22},{16,24},... | collective-permute-start | bytes 4718600 | tf_op jit(solution)/shard_map/ppermute | solution.py:19
  159.9 70.7 %collective-permute-start.3 = (bf16[8,2,4,384,128]{4,3,2,1,0:T(8,128)(2,1)}, bf16[8,2,4,384,128]{4,3,2,1,0:T(8,128)(2,1)}, u32[]{:S(2)}, u32[]{:S(2)}) collective-permute-start(bf16[8,2,4,384,128]{4,3,2,1,0:T(8,128)(2,1)} %get-tuple-element.19), channel_id=1, source_target_pairs={{2,0},{4,2},{6,4},{8,6},{10,8},{12,10},{14,12},{16,14},{18,16},{20... | collective-permute-start | bytes 18874376 | tf_op jit(solution)/shard_map/ppermute | solution.py:19
  161.9 139.2 %collective-permute-start.2 = (bf16[8,2,4,384,128]{4,3,2,1,0:T(8,128)(2,1)}, bf16[8,2,4,384,128]{4,3,2,1,0:T(8,128)(2,1)}, u32[]{:S(2)}, u32[]{:S(2)}) collective-permute-start(bf16[8,2,4,384,128]{4,3,2,1,0:T(8,128)(2,1)} %get-tuple-element.19), channel_id=1, source_target_pairs={{0,2},{2,4},{4,6},{6,8},{8,10},{10,12},{12,14},{14,16},{16,18},{18... | collective-permute-start | bytes 18874376 | tf_op jit(solution)/shard_map/ppermute | solution.py:19
  164.7 136.4 %copy-start.3 = (bf16[8,2,1,4,384,128]{5,4,3,2,1,0:T(8,128)(2,1)S(1)}, bf16[8,2,1,4,384,128]{5,4,3,2,1,0:T(8,128)(2,1)}, u32[]{:S(2)}) copy-start(bf16[8,2,1,4,384,128]{5,4,3,2,1,0:T(8,128)(2,1)} %get-tuple-element.18) | copy-start | bytes 18874372
  378.9 70.4 %collective-permute-start.4 = (bf16[8,2,4,384,128]{4,3,2,1,0:T(8,128)(2,1)S(1)}, bf16[8,2,4,384,128]{4,3,2,1,0:T(8,128)(2,1)S(1)}, u32[]{:S(2)}, u32[]{:S(2)}) collective-permute-start(bf16[8,2,4,384,128]{4,3,2,1,0:T(8,128)(2,1)S(1)} %slice_bitcast_fusion), channel_id=1, source_target_pairs={{2,0},{4,2},{6,4},{8,6},{10,8},{12,10},{14,12},{16,14},{18,16},{20... | collective-permute-start | bytes 18874376 | tf_op jit(solution)/shard_map/ppermute | solution.py:19
  380.9 72.4 %collective-permute-start.5 = (bf16[8,2,4,384,128]{4,3,2,1,0:T(8,128)(2,1)S(1)}, bf16[8,2,4,384,128]{4,3,2,1,0:T(8,128)(2,1)}, u32[]{:S(2)}, u32[]{:S(2)}) collective-permute-start(bf16[8,2,4,384,128]{4,3,2,1,0:T(8,128)(2,1)S(1)} %slice_bitcast_fusion.2), channel_id=1, source_target_pairs={{0,2},{2,4},{4,6},{6,8},{8,10},{10,12},{12,14},{14,16},{16,18},{18... | collective-permute-start | bytes 18874376 | tf_op jit(solution)/shard_map/ppermute | solution.py:19
  449.3 2.6 copy-start.4
  462.1 89.1 %collective-permute-start.6 = (bf16[8,2,384,128]{3,2,1,0:T(8,128)(2,1)S(1)}, bf16[8,2,384,128]{3,2,1,0:T(8,128)(2,1)S(1)}, u32[]{:S(2)}, u32[]{:S(2)}) collective-permute-start(bf16[8,2,384,128]{3,2,1,0:T(8,128)(2,1)S(1)} %get-tuple-element.16), channel_id=1, source_target_pairs={{0,8},{2,10},{4,12},{6,14},{8,16},{10,18},{12,20},{14,22},{16,24},... | collective-permute-start | bytes 4718600 | tf_op jit(solution)/shard_map/ppermute | solution.py:19
  533.4 22.6 %collective-permute-start.7 = (bf16[8,2,384,128]{3,2,1,0:T(8,128)(2,1)S(1)}, bf16[8,2,384,128]{3,2,1,0:T(8,128)(2,1)S(1)}, u32[]{:S(2)}, u32[]{:S(2)}) collective-permute-start(bf16[8,2,384,128]{3,2,1,0:T(8,128)(2,1)S(1)} %get-tuple-element.17), channel_id=1, source_target_pairs={{8,0},{10,2},{12,4},{14,6},{16,8},{18,10},{20,12},{22,14},{24,16},... | collective-permute-start | bytes 4718600 | tf_op jit(solution)/shard_map/ppermute | solution.py:19
  636.0 6.6 %copy-start.1 = (s32[16,2]{0,1:T(2,128)S(1)}, s32[16,2]{0,1:T(2,128)}, u32[]{:S(2)}) copy-start(s32[16,2]{0,1:T(2,128)} %param.9) | copy-start | bytes 388
